TPU v7x, 512 devices: a whole 4x4x16 slice. The times are simulated.
512 devices in a mesh: row: 16 (over z), col: 32 (over y, x, core).
Axes of the slice: x: 4, y: 4, z: 16, core: 2. Of those that a mesh axis runs over, the one named last changes fastest.
Arguments:
- centroids: float32 [3, 32768], P(None, ('col', 'row')), may hold values from 0 to 1, as said below
- areas: float32 [32768], P(('col', 'row')), may hold values from 0.5 to 2
- conductance: float32 [32768], P(('col', 'row')), may hold values from 0.1 to 1
- power: float32 [16, 32768], P(None, ('col', 'row')), may hold values from -3 to 6
Outputs:
- solution: float32 [16, 32768], P(None, ('col', 'row'))
- residual: float32 [16, 32768], P(None, ('col', 'row'))
Inputs may be any that keep to these rules, and one draw needn't show every extreme that they name: `centroids`: panels lie on 16 parallel fins across the unit cube.
All inputs are finite; a program needn't handle non-finite values.
Results may differ from a plain program's by a relative error of at most 0.00039.
Values may be sent and summed in bfloat16 or wider, within the bound.
No kernel may reach another device: no remote copies, remote signals or barrier semaphores. Data moves between devices by JAX's collectives and lax.ppermute only.
A program may use at most 64 MiB of HBM per device.

v0:
```python
import math
import jax
import jax.numpy as jnp
from jax import lax
from jax.sharding import PartitionSpec as P


def kernel_tile(src, tgt, scale, delta2):
    dx = src[0][:, None] - tgt[0][None, :]
    dy = src[1][:, None] - tgt[1][None, :]
    dz = src[2][:, None] - tgt[2][None, :]
    dist2 = dx * dx + dy * dy + dz * dz
    return (src[3][:, None] * scale * lax.rsqrt(dist2 + delta2)).astype(jnp.bfloat16)


def inner(left, right):
    return jnp.dot(left, right.T, precision=lax.Precision.HIGHEST)


def lower_inverse(gram):
    factor = jnp.linalg.cholesky(gram)
    eye = jnp.eye(gram.shape[0], dtype=jnp.float32)
    return (factor, jax.scipy.linalg.solve_triangular(factor, eye, lower=True))


def reduce_small(terms):
    return lax.psum(terms, ("row", "col"))


def body(centroids, areas, conductance, power):
    high = lax.Precision.HIGHEST
    width = power.shape[1]
    nrhs = power.shape[0]
    panels = width * lax.axis_size("row") * lax.axis_size("col")
    scale = 4.0 / (math.pi * panels)
    delta2 = 16.0 / panels
    geom = jnp.concatenate([centroids, areas[None, :]], 0)
    sources = lax.all_gather(geom, "col", axis=1, tiled=True)
    targets = lax.all_gather(centroids, "row", axis=1, tiled=True)
    tgt_len = targets.shape[1]
    rhs, cond_row = (power, conductance[None, :])
    factor0, inverse0 = lower_inverse(reduce_small(inner(rhs, rhs)))
    basis = [jnp.dot(inverse0, rhs, precision=high)]
    blocks = {}
    for step in range(2):
        field = basis[step]
        empty = jnp.zeros((nrhs, tgt_len), jnp.float32)
        piece = lax.all_gather(field.astype(jnp.bfloat16), "col", axis=1, tiled=True)
        cols = piece.shape[1]
        step_len = width * max(1, 512 // width)
        turns = cols // step_len

        def one(turn, acc):
            vec = lax.dynamic_slice_in_dim(piece, turn * step_len, step_len, 1)
            src = lax.dynamic_slice_in_dim(sources, turn * step_len, step_len, 1)
            tile = kernel_tile(src, targets, scale, delta2)
            return acc + jnp.dot(vec, tile, preferred_element_type=jnp.float32)

        apply_total = lax.fori_loop(0, turns, one, empty)
        product = lax.psum_scatter(apply_total, "row", scatter_dimension=1, tiled=True)
        image = cond_row * field + product
        coeffs = list(reduce_small(tuple((inner(vec, image) for vec in basis))))
        for idx in range(step + 1):
            image = image - jnp.dot(coeffs[idx].T, basis[idx], precision=high)
        gram = reduce_small(inner(image, image))
        for idx in range(step + 1):
            blocks[idx, step] = coeffs[idx]
        factor, inverse = lower_inverse(gram)
        blocks[step + 1, step] = factor.T
        basis.append(jnp.dot(inverse, image, precision=high))
    hbar = jnp.zeros((3 * nrhs, 2 * nrhs), jnp.float32)
    for key in blocks:
        hbar = hbar.at[
            key[0] * nrhs : (key[0] + 1) * nrhs, key[1] * nrhs : (key[1] + 1) * nrhs
        ].set(blocks[key])
    target = jnp.zeros((3 * nrhs, nrhs), jnp.float32).at[:nrhs].set(factor0.T)
    normal = jnp.dot(hbar.T, hbar, precision=high)
    chol = jnp.linalg.cholesky(normal)
    coeff_y = jax.scipy.linalg.cho_solve((chol, True), jnp.dot(hbar.T, target, precision=high))
    coeff_z = target - jnp.dot(hbar, coeff_y, precision=high)
    solution = jnp.dot(coeff_y[:nrhs].T, basis[0], precision=high) + jnp.dot(
        coeff_y[nrhs:].T, basis[1], precision=high
    )
    residual = jnp.dot(coeff_z[:nrhs].T, basis[0], precision=high) + jnp.dot(
        coeff_z[nrhs : 2 * nrhs].T, basis[1], precision=high
    )
    residual = residual + jnp.dot(coeff_z[2 * nrhs :].T, basis[2], precision=high)
    return (solution, residual)


def solution(mesh):
    return jax.shard_map(
        body,
        mesh=mesh,
        in_specs=(
            P(None, ("col", "row")),
            P(("col", "row")),
            P(("col", "row")),
            P(None, ("col", "row")),
        ),
        out_specs=(P(None, ("col", "row")), P(None, ("col", "row"))),
        check_vma=False,
    )
```

profile of v0, /device:TPU:1, one launch (start us, length us, event | category | flops | bytes accessed | tf_op | source)
XLA Modules:
  0.0 797.1 jit_solution(8880030113008817273)
XLA Ops:
  7.3 0.6 copy-done
  8.0 111.0 %psum.42 = f32[16,16]{0,1:T(8,128)S(1)} all-reduce(f32[16,16]{0,1:T(8,128)S(1)} %fusion.59), channel_id=1, replica_groups=mesh['row'=16,'col'=32] {'row','col'}, use_global_device_ids=true, to_apply=%region_0.0 | all-reduce | flops 256 | bytes 2048 | tf_op jit(solution)/shard_map/psum | solution.py:27
  119.1 1.5 cholesky.94
  120.6 0.6 compare_reduce_fusion.2
  121.3 0.6 fusion.49
  121.9 1.2 custom-call.20
  123.1 0.2 fusion.30
  123.5 22.9 %all-gather = bf16[32,64,16]{1,2,0:T(8,128)(2,1)S(1)} all-gather(bf16[1,64,16]{1,2,0:T(8,128)(2,1)S(1)} %convert_bitcast_fusion.1), channel_id=1, replica_groups=mesh['row'=16,'col'=32] {'col'}, dimensions={0}, use_global_device_ids=true | all-gather | bytes 67584 | tf_op jit(solution)/shard_map/all_gather | solution.py:48
  146.5 0.2 reshape.234
  146.7 23.6 %all-gather.1 = f32[32,64,4]{1,2,0:T(4,128)S(1)} all-gather(f32[1,64,4]{1,2,0:T(4,128)S(1)} %maximum_bitcast_fusion), channel_id=1, replica_groups=mesh['row'=16,'col'=32] {'col'}, dimensions={0}, use_global_device_ids=true | all-gather | bytes 33792 | tf_op jit(solution)/shard_map/all_gather | solution.py:38
  170.4 19.9 %all-gather.2 = f32[16,64,3]{1,2,0:T(4,128)S(1)} all-gather(f32[1,64,3]{1,2,0:T(4,128)S(1)} %bitcast.175), channel_id=1, replica_groups=mesh['row'=16,'col'=32] {'row'}, dimensions={0}, use_global_device_ids=true | all-gather | bytes 13056 | tf_op jit(solution)/shard_map/all_gather | solution.py:39
  190.4 4.5 while.34
  190.5 1.0 convolution_add_fusion.7
  191.6 1.0 convolution_add_fusion.7
  192.8 1.0 convolution_add_fusion.7
  193.9 1.0 convolution_add_fusion.7
  194.9 1.0 copy.57
  196.0 59.8 %reduce-scatter.7.cloned.1.call-done = f32[64,16]{1,0:T(8,128)} async-done(((f32[1024,16]{1,0:T(8,128)}), f32[64,16]{1,0:T(8,128)}) %reduce-scatter.7.cloned.1.call-update) | async-done | bytes 4112
  255.8 0.8 copy.58
  256.7 111.7 %psum.43 = f32[16,16]{1,0:T(8,128)S(1)} all-reduce(f32[16,16]{1,0:T(8,128)S(1)} %fusion.46), channel_id=1, replica_groups=mesh['row'=16,'col'=32] {'row','col'}, use_global_device_ids=true, to_apply=%region_6.0 | all-reduce | flops 256 | bytes 2048 | tf_op jit(solution)/shard_map/psum | solution.py:27
  368.4 0.2 convolution_subtract_fusion.3
  368.7 100.0 %psum.44 = f32[16,16]{0,1:T(8,128)S(1)} all-reduce(f32[16,16]{0,1:T(8,128)S(1)} %fusion.61), channel_id=1, replica_groups=mesh['row'=16,'col'=32] {'row','col'}, use_global_device_ids=true, to_apply=%region_7.0 | all-reduce | flops 256 | bytes 2048 | tf_op jit(solution)/shard_map/psum | solution.py:27
  468.8 1.5 cholesky.105
  470.3 0.6 compare_reduce_fusion.1
  470.9 0.6 select_bitcast_fusion.1
  471.6 1.2 custom-call.21
  472.8 0.2 fusion.28
  473.2 24.4 %all-gather.3 = bf16[32,64,16]{1,2,0:T(8,128)(2,1)S(1)} all-gather(bf16[1,64,16]{1,2,0:T(8,128)(2,1)S(1)} %convert_bitcast_fusion), channel_id=1, replica_groups=mesh['row'=16,'col'=32] {'col'}, dimensions={0}, use_global_device_ids=true | all-gather | bytes 67584 | tf_op jit(solution)/shard_map/all_gather | solution.py:48
  497.6 0.2 reshape.240
  497.7 4.5 while.35
  497.9 1.0 convolution_add_fusion.8
  499.0 1.0 convolution_add_fusion.8
  500.1 1.0 convolution_add_fusion.8
  501.2 1.0 convolution_add_fusion.8
  502.3 1.0 copy.59
  503.3 0.6 fusion.58
  503.9 0.7 and_reduce_fusion
  504.6 0.5 scatter.21
  505.2 51.2 %reduce-scatter.9.cloned.1.call-done = f32[64,16]{1,0:T(8,128)} async-done(((f32[1024,16]{1,0:T(8,128)}), f32[64,16]{1,0:T(8,128)}) %reduce-scatter.9.cloned.1.call-update) | async-done | bytes 4112
  556.4 0.8 copy.60
  557.5 111.9 %all-reduce.2 = (f32[16,16]{1,0:T(8,128)S(1)}, f32[16,16]{1,0:T(8,128)S(1)}) all-reduce(f32[16,16]{1,0:T(8,128)S(1)} %fusion.54, f32[16,16]{1,0:T(8,128)S(1)} %fusion.53), channel_id=1, replica_groups=mesh['row'=16,'col'=32] {'row','col'}, use_global_device_ids=true, to_apply=%region_12.0 | all-reduce | flops 512 | bytes 4096 | tf_op jit(solution)/shard_map/psum | solution.py:27
  669.4 0.2 convolution_subtract_fusion.2
  669.6 0.2 convolution_subtract_fusion.1
  669.9 100.3 %psum.47 = f32[16,16]{0,1:T(8,128)S(1)} all-reduce(f32[16,16]{0,1:T(8,128)S(1)} %fusion.63), channel_id=1, replica_groups=mesh['row'=16,'col'=32] {'row','col'}, use_global_device_ids=true, to_apply=%region_14.0 | all-reduce | flops 256 | bytes 2048 | tf_op jit(solution)/shard_map/psum | solution.py:27
  770.3 1.5 cholesky.116
  771.8 0.7 compare_reduce_fusion
  772.5 0.7 select_bitcast_fusion
  773.3 2.0 dynamic-slice_select_fusion
  775.3 2.1 scatter.24
  777.4 0.8 scatter.25
  778.2 0.7 scatter.26
  779.0 0.2 fusion.64
  779.3 2.9 cholesky.41
  782.2 0.6 compare_reduce_fusion.3
  782.9 0.7 fusion.20
  783.5 2.4 custom-call.15
  786.0 0.2 fusion.47
  786.4 0.2 convolution_subtract_fusion
  786.6 0.1 fusion.37
  786.7 1.2 custom-call.22
  788.0 0.2 fusion.26
  788.4 0.2 convolution_add_fusion.3
  788.7 0.8 convolution_add_fusion.4
  789.5 0.8 convolution_add_fusion.2
  (68 shorter events, 3.4 us)
Async XLA Ops:
  7.2 0.7 copy-start
  7.2 139.5 %copy-start.3 = (f32[64]{0:T(128)S(1)}, f32[64]{0:T(128)}, u32[]{:S(2)}) copy-start(f32[64]{0:T(128)} %param.24) | copy-start | bytes 772
  7.2 139.5 %copy-start.2 = (f32[3,64]{1,0:T(4,128)S(1)}, f32[3,64]{1,0:T(4,128)}, u32[]{:S(2)}) copy-start(f32[3,64]{1,0:T(4,128)} %param.23) | copy-start | bytes 2308
  7.2 248.6 %reduce-scatter.7.cloned.1.call-start = ((), (), s32[]{:S(2)}) async-start(), calls=%async_computation.2 | async-start | bytes 557056
  194.9 61.7 %copy-start.1 = (f32[64]{0:T(128)S(1)}, f32[64]{0:T(128)}, u32[]{:S(2)}) copy-start(f32[64]{0:T(128)} %param.25) | copy-start | bytes 772
  195.9 360.5 %reduce-scatter.9.cloned.1.call-start = ((), (), s32[]{:S(2)}) async-start(), calls=%async_computation.3 | async-start | bytes 557056
  502.3 1.6 copy-start.4
Sparse Core Ops, SparseCore 0:
  196.0 59.6 reduce-scatter.6
  503.4 52.9 reduce-scatter.8
where the time goes:
time: 798 us; the launch traced here: 797 us
  blocking collectives  626 us (78%)
  waiting for transfers between devices  111 us (14%)
  other arithmetic  22.3 us (3%)
  between operations  14.2 us (2%)
  matrix products  13.4 us (2%)
  local copies, waits for them, and re-layouts  10.1 us (1%)
    psum x5, blocking collectives, reduce_small(): return lax.psum(terms, ('row', 'col'))  535 us
    unnamed x4, waiting for transfers between devices  111 us
    all_gather x2, blocking collectives, body(): lax.all_gather(field.astype(jnp.bfloat16), 'col', axis=1, tiled=True)  47.3 us
    all_gather x1, blocking collectives, body(): sources = lax.all_gather(geom, 'col', axis=1, tiled=True)  23.6 us
    all_gather x1, blocking collectives, body(): targets = lax.all_gather(centroids, 'row', axis=1, tiled=True)  19.9 us
  transfers between devices with their start and end apart: 2, of which 2 were waited for; matrix products, arithmetic and copies ran while one was open for 0% of the time, Pallas kernels for 0%

commit v1 on v0

--- a/solution.py
+++ b/solution.py
@@ -3,6 +3,11 @@
 import jax.numpy as jnp
 from jax import lax
 from jax.sharding import PartitionSpec as P
+
+
+def axis_by_axis(x, one_2, other):
+    partial = lax.psum(x, one_2)
+    return lax.psum(partial, other)
 
 
 def kernel_tile(src, tgt, scale, delta2):
@@ -24,7 +29,7 @@
 
 
 def reduce_small(terms):
-    return lax.psum(terms, ("row", "col"))
+    return axis_by_axis(terms, "col", "row")
 
 
 def body(centroids, areas, conductance, power):

time: 798 us -> 842 us (1.055)
  blocking collectives: 626 us -> 663 us
    psum x5 -> x10, blocking collectives: 535 us -> 557 us  [the longest x5 427 us: axis_by_axis(): partial = lax.psum(x, one_2)]
    all_gather x2, blocking collectives: 47.3 us -> 61.3 us  [body(): lax.all_gather(field.astype(jnp.bfloat16), 'col', axis=1, tiled=True)]
where the time goes in v1:
time: 842 us; the launch traced here: 835 us
  blocking collectives  663 us (79%)
  waiting for transfers between devices  112 us (13%)
  other arithmetic  22.3 us (3%)
  between operations  14.3 us (2%)
  matrix products  13.4 us (2%)
  local copies, waits for them, and re-layouts  10.1 us (1%)
    psum x5, blocking collectives, axis_by_axis(): partial = lax.psum(x, one_2)  427 us
    psum x5, blocking collectives, axis_by_axis(): return lax.psum(partial, other)  130 us
    unnamed x4, waiting for transfers between devices  112 us
    all_gather x2, blocking collectives, body(): lax.all_gather(field.astype(jnp.bfloat16), 'col', axis=1, tiled=True)  61.3 us
    all_gather x1, blocking collectives, body(): sources = lax.all_gather(geom, 'col', axis=1, tiled=True)  25.1 us
    all_gather x1, blocking collectives, body(): targets = lax.all_gather(centroids, 'row', axis=1, tiled=True)  19.1 us
  transfers between devices with their start and end apart: 2, of which 2 were waited for; matrix products, arithmetic and copies ran while one was open for 0% of the time, Pallas kernels for 0%

profile of v1, /device:TPU:1, one launch (start us, length us, event | category | flops | bytes accessed | tf_op | source)
XLA Modules:
  0.0 835.3 jit_solution(14596988230392864560)
XLA Ops:
  7.3 0.6 copy-done
  8.0 69.9 %psum.84 = f32[16,16]{0,1:T(8,128)S(1)} all-reduce(f32[16,16]{0,1:T(8,128)S(1)} %fusion.59), channel_id=1, replica_groups=mesh['row'=16,'col'=32] {'col'}, use_global_device_ids=true, to_apply=%region_0.0 | all-reduce | flops 256 | bytes 2048 | tf_op jit(solution)/shard_map/psum | solution.py:9
  77.9 24.7 %psum.85 = f32[16,16]{0,1:T(8,128)S(1)} all-reduce(f32[16,16]{0,1:T(8,128)S(1)} %psum.84), channel_id=1, replica_groups=mesh['row'=16,'col'=32] {'row'}, use_global_device_ids=true, to_apply=%region_1.0 | all-reduce | flops 256 | bytes 2048 | tf_op jit(solution)/shard_map/psum | solution.py:10
  102.6 1.5 cholesky.94
  104.1 0.6 compare_reduce_fusion.2
  104.8 0.6 fusion.49
  105.4 1.2 custom-call.20
  106.7 0.2 fusion.30
  107.0 32.9 %all-gather = bf16[32,64,16]{1,2,0:T(8,128)(2,1)S(1)} all-gather(bf16[1,64,16]{1,2,0:T(8,128)(2,1)S(1)} %convert_bitcast_fusion.1), channel_id=1, replica_groups=mesh['row'=16,'col'=32] {'col'}, dimensions={0}, use_global_device_ids=true | all-gather | bytes 67584 | tf_op jit(solution)/shard_map/all_gather | solution.py:53
  140.2 25.1 %all-gather.1 = f32[32,64,4]{1,2,0:T(4,128)S(1)} all-gather(f32[1,64,4]{1,2,0:T(4,128)S(1)} %maximum_bitcast_fusion), channel_id=1, replica_groups=mesh['row'=16,'col'=32] {'col'}, dimensions={0}, use_global_device_ids=true | all-gather | bytes 33792 | tf_op jit(solution)/shard_map/all_gather | solution.py:43
  165.4 19.1 %all-gather.2 = f32[16,64,3]{1,2,0:T(4,128)S(1)} all-gather(f32[1,64,3]{1,2,0:T(4,128)S(1)} %bitcast.175), channel_id=1, replica_groups=mesh['row'=16,'col'=32] {'row'}, dimensions={0}, use_global_device_ids=true | all-gather | bytes 13056 | tf_op jit(solution)/shard_map/all_gather | solution.py:44
  184.6 4.5 while.34
  184.7 1.0 convolution_add_fusion.7
  185.8 1.0 convolution_add_fusion.7
  186.9 1.0 convolution_add_fusion.7
  188.1 1.0 convolution_add_fusion.7
  189.1 1.0 copy.57
  190.2 58.7 %reduce-scatter.7.cloned.1.call-done = f32[64,16]{1,0:T(8,128)} async-done(((f32[1024,16]{1,0:T(8,128)}), f32[64,16]{1,0:T(8,128)}) %reduce-scatter.7.cloned.1.call-update) | async-done | bytes 4112
  248.9 0.8 copy.58
  249.8 74.7 %psum.86 = f32[16,16]{1,0:T(8,128)S(1)} all-reduce(f32[16,16]{1,0:T(8,128)S(1)} %fusion.46), channel_id=1, replica_groups=mesh['row'=16,'col'=32] {'col'}, use_global_device_ids=true, to_apply=%region_7.0 | all-reduce | flops 256 | bytes 2048 | tf_op jit(solution)/shard_map/psum | solution.py:9
  324.5 22.0 %psum.87 = f32[16,16]{1,0:T(8,128)S(1)} all-reduce(f32[16,16]{1,0:T(8,128)S(1)} %psum.86), channel_id=1, replica_groups=mesh['row'=16,'col'=32] {'row'}, use_global_device_ids=true, to_apply=%region_8.0 | all-reduce | flops 256 | bytes 2048 | tf_op jit(solution)/shard_map/psum | solution.py:10
  346.5 0.2 convolution_subtract_fusion.3
  346.8 70.7 %psum.88 = f32[16,16]{0,1:T(8,128)S(1)} all-reduce(f32[16,16]{0,1:T(8,128)S(1)} %fusion.61), channel_id=1, replica_groups=mesh['row'=16,'col'=32] {'col'}, use_global_device_ids=true, to_apply=%region_9.0 | all-reduce | flops 256 | bytes 2048 | tf_op jit(solution)/shard_map/psum | solution.py:9
  417.5 22.2 %psum.89 = f32[16,16]{0,1:T(8,128)S(1)} all-reduce(f32[16,16]{0,1:T(8,128)S(1)} %psum.88), channel_id=1, replica_groups=mesh['row'=16,'col'=32] {'row'}, use_global_device_ids=true, to_apply=%region_10.0 | all-reduce | flops 256 | bytes 2048 | tf_op jit(solution)/shard_map/psum | solution.py:10
  439.8 1.5 cholesky.105
  441.3 0.6 compare_reduce_fusion.1
  442.0 0.6 select_bitcast_fusion.1
  442.6 1.2 custom-call.21
  443.8 0.2 fusion.28
  444.2 28.4 %all-gather.3 = bf16[32,64,16]{1,2,0:T(8,128)(2,1)S(1)} all-gather(bf16[1,64,16]{1,2,0:T(8,128)(2,1)S(1)} %convert_bitcast_fusion), channel_id=1, replica_groups=mesh['row'=16,'col'=32] {'col'}, dimensions={0}, use_global_device_ids=true | all-gather | bytes 67584 | tf_op jit(solution)/shard_map/all_gather | solution.py:53
  472.8 4.5 while.35
  472.9 1.0 convolution_add_fusion.8
  474.1 1.0 convolution_add_fusion.8
  475.2 1.0 convolution_add_fusion.8
  476.3 1.0 convolution_add_fusion.8
  477.3 1.0 copy.59
  478.3 0.6 fusion.58
  478.9 0.7 and_reduce_fusion
  479.7 0.5 scatter.21
  480.2 53.5 %reduce-scatter.9.cloned.1.call-done = f32[64,16]{1,0:T(8,128)} async-done(((f32[1024,16]{1,0:T(8,128)}), f32[64,16]{1,0:T(8,128)}) %reduce-scatter.9.cloned.1.call-update) | async-done | bytes 4112
  533.7 0.8 copy.60
  534.8 129.5 %all-reduce.2 = (f32[16,16]{1,0:T(8,128)S(1)}, f32[16,16]{1,0:T(8,128)S(1)}) all-reduce(f32[16,16]{1,0:T(8,128)S(1)} %fusion.54, f32[16,16]{1,0:T(8,128)S(1)} %fusion.53), channel_id=1, replica_groups=mesh['row'=16,'col'=32] {'col'}, use_global_device_ids=true, to_apply=%region_15.0 | all-reduce | flops 512 | bytes 4096 | tf_op jit(solution)/shard_map/psum | solution.py:9
  664.3 40.4 %all-reduce.3 = (f32[16,16]{1,0:T(8,128)S(1)}, f32[16,16]{1,0:T(8,128)S(1)}) all-reduce(f32[16,16]{1,0:T(8,128)S(1)} %get-tuple-element.322, f32[16,16]{1,0:T(8,128)S(1)} %get-tuple-element.323), channel_id=1, replica_groups=mesh['row'=16,'col'=32] {'row'}, use_global_device_ids=true, to_apply=%region_16.0 | all-reduce | flops 512 | bytes 4096 | tf_op jit(solution)/shard_map/psum | solution.py:10
  704.7 0.2 convolution_subtract_fusion.2
  704.9 0.2 convolution_subtract_fusion.1
  705.2 82.1 %psum.94 = f32[16,16]{0,1:T(8,128)S(1)} all-reduce(f32[16,16]{0,1:T(8,128)S(1)} %fusion.63), channel_id=1, replica_groups=mesh['row'=16,'col'=32] {'col'}, use_global_device_ids=true, to_apply=%region_19.0 | all-reduce | flops 256 | bytes 2048 | tf_op jit(solution)/shard_map/psum | solution.py:9
  787.3 21.1 %psum.95 = f32[16,16]{0,1:T(8,128)S(1)} all-reduce(f32[16,16]{0,1:T(8,128)S(1)} %psum.94), channel_id=1, replica_groups=mesh['row'=16,'col'=32] {'row'}, use_global_device_ids=true, to_apply=%region_20.0 | all-reduce | flops 256 | bytes 2048 | tf_op jit(solution)/shard_map/psum | solution.py:10
  808.5 1.5 cholesky.116
  810.0 0.7 compare_reduce_fusion
  810.7 0.7 select_bitcast_fusion
  811.5 2.0 dynamic-slice_select_fusion
  813.5 2.1 scatter.24
  815.6 0.8 scatter.25
  816.4 0.7 scatter.26
  817.2 0.2 fusion.64
  817.5 2.9 cholesky.41
  820.4 0.6 compare_reduce_fusion.3
  821.1 0.7 fusion.20
  821.7 2.4 custom-call.15
  824.9 1.2 custom-call.22
  826.2 0.2 fusion.26
  826.7 0.2 convolution_add_fusion.3
  826.9 0.8 convolution_add_fusion.4
  827.7 0.8 convolution_add_fusion.2
  (73 shorter events, 4.2 us)
Async XLA Ops:
  7.2 0.7 copy-start
  7.2 133.0 %copy-start.3 = (f32[64]{0:T(128)S(1)}, f32[64]{0:T(128)}, u32[]{:S(2)}) copy-start(f32[64]{0:T(128)} %param.24) | copy-start | bytes 772
  7.2 133.0 %copy-start.2 = (f32[3,64]{1,0:T(4,128)S(1)}, f32[3,64]{1,0:T(4,128)}, u32[]{:S(2)}) copy-start(f32[3,64]{1,0:T(4,128)} %param.23) | copy-start | bytes 2308
  7.2 241.7 %reduce-scatter.7.cloned.1.call-start = ((), (), s32[]{:S(2)}) async-start(), calls=%async_computation.2 | async-start | bytes 557056
  189.1 60.6 %copy-start.1 = (f32[64]{0:T(128)S(1)}, f32[64]{0:T(128)}, u32[]{:S(2)}) copy-start(f32[64]{0:T(128)} %param.25) | copy-start | bytes 772
  190.1 343.6 %reduce-scatter.9.cloned.1.call-start = ((), (), s32[]{:S(2)}) async-start(), calls=%async_computation.3 | async-start | bytes 557056
  477.3 1.6 copy-start.4
Sparse Core Ops, SparseCore 0:
  190.2 58.5 reduce-scatter.6
  478.5 55.1 reduce-scatter.8
